TPU v7x, 32 devices: a whole 2x2x4 slice. The times are simulated.
32 devices in a mesh: groups: 2 (over y), row: 4 (over z), col: 4 (over x, core).
Axes of the slice: x: 2, y: 2, z: 4, core: 2. Of those that a mesh axis runs over, the one named last changes fastest.
Arguments:
- left_tiles: bfloat16 [4096, 5120], P(('groups', 'row'), 'col'), parts along dimension 0, may hold values from -6 to 6
- right_tiles: bfloat16 [10240, 3072], P(('groups', 'row'), 'col'), parts along dimension 0, may hold values from -0.375 to 0.375
- left_blocks: int32 [8, 4, 10], P(('groups', 'row'), 'col'), parts along dimension 0, may hold values from 0 to 9, each once within a row
- left_count: int32 [8, 4], P(('groups', 'row'), 'col'), parts along dimension 0, may hold values from 0 to 4, as said below
- right_blocks: int32 [8, 4, 15], P(('groups', 'row'), 'col'), parts along dimension 0, may hold values from 0 to 14, each once within a row
- right_count: int32 [8, 4], P(('groups', 'row'), 'col'), parts along dimension 0, may hold values from 0 to 4, as said below
Outputs:
- partial_square: float32 [4096, 3072], P(('groups', 'row'), 'col'), parts along dimension 0
There are 2 independent parts, one for each index of `groups`. A program takes and returns all parts, laid end to end along the dimension named above; each array names one. Nothing has to cross between parts.
Inputs may be any that keep to these rules, and one draw needn't show every extreme that they name: `left_blocks`: each tile's entries name every block number of the tile once; the first left_count entries are the occupied blocks. `left_count`: at most 4 occupied blocks in a tile; some tile has exactly 4 in every draw. `right_blocks`: each tile's entries name every block number of the tile once; the first right_count entries are the occupied blocks. `right_count`: at most 4 occupied blocks in a tile; some tile has exactly 4 in every draw.
All inputs are finite; a program needn't handle non-finite values.
Results may differ from a plain program's by a relative error of at most 0.0003.
Values may be sent and summed in bfloat16 or wider, within the bound.
A program may use at most 64 MiB of HBM per device.

v0:
```python
import jax
import jax.numpy as jnp
from jax import lax
from jax.sharding import PartitionSpec as P

BW = 256
STEPS = 4


def passed_along(block, axis, distance):
    devices = range(lax.axis_size(axis))
    route = [((i - distance) % len(devices), i) for i in devices]
    return lax.ppermute(block, axis, route)


def masked(tile, listing, occupied, block_rows, block_cols):
    slot_total = listing.shape[2]
    block_index = jnp.arange(block_rows * block_cols, dtype=jnp.int32)
    slot_index = jnp.arange(slot_total, dtype=jnp.int32)
    hits = (listing[0, 0, :, None] == block_index[None, :]) & (slot_index[:, None] < occupied[0, 0])
    keep_mask = jnp.sum(hits.astype(jnp.float32), axis=0).astype(tile.dtype)
    shaped = tile.reshape(block_rows, BW, block_cols, BW) * keep_mask.reshape(
        block_rows, 1, block_cols, 1
    )
    return shaped.reshape(tile.shape)


def on_device(left_tiles, right_tiles, left_blocks, left_count, right_blocks, right_count):
    left_rows = left_tiles.shape[0] // BW
    inner_blocks = left_tiles.shape[1] // BW
    right_cols = right_tiles.shape[1] // BW
    total = jnp.zeros((left_tiles.shape[0], right_tiles.shape[1]), jnp.float32)
    held_left = (left_tiles, left_blocks, left_count)
    held_right = (right_tiles, right_blocks, right_count)
    for step in range(STEPS):
        total = total + jnp.dot(
            masked(held_left[0], held_left[1], held_left[2], left_rows, inner_blocks),
            masked(held_right[0], held_right[1], held_right[2], inner_blocks, right_cols),
            preferred_element_type=jnp.float32,
        )
        if step + 1 < STEPS:
            held_left = passed_along((held_left[0], held_left[1], held_left[2]), "col", -1)
            held_right = passed_along((held_right[0], held_right[1], held_right[2]), "row", -1)
    return total


def solution(mesh):
    placed = (
        P(("groups", "row"), "col"),
        P(("groups", "row"), "col"),
        P(("groups", "row"), "col", None),
        P(("groups", "row"), "col"),
        P(("groups", "row"), "col", None),
        P(("groups", "row"), "col"),
    )
    return jax.shard_map(
        on_device,
        mesh=mesh,
        in_specs=placed,
        out_specs=P(("groups", "row"), "col"),
        check_vma=False,
    )
```

profile of v0, /device:TPU:0, one launch (start us, length us, event | category | flops | bytes accessed | tf_op | source)
XLA Modules:
  0.0 186.3 jit_solution(12033582798532226025)
XLA Ops:
  0.0 5.0 %collective-permute-start.3 = (bf16[1280,768]{1,0:T(8,128)(2,1)}, bf16[1280,768]{1,0:T(8,128)(2,1)}, u32[]{:S(2)}, u32[]{:S(2)}) collective-permute-start(bf16[1280,768]{1,0:T(8,128)(2,1)} %param.7), channel_id=1, source_target_pairs={{4,0},{8,4},{12,8},{0,12},{5,1},{9,5},{13,9},{1,13},{6,2},{10,6},{... | collective-permute-start | bytes 5898248 | tf_op jit(solution)/shard_map/ppermute | solution.py:13
  5.1 1.6 copy.14
  7.4 40.1 %collective-permute-done.3 = bf16[1280,768]{1,0:T(8,128)(2,1)} collective-permute-done((bf16[1280,768]{1,0:T(8,128)(2,1)}, bf16[1280,768]{1,0:T(8,128)(2,1)}, u32[]{:S(2)}, u32[]{:S(2)}) %collective-permute-start.3) | collective-permute-done | bytes 1966112 | tf_op jit(solution)/shard_map/ppermute | solution.py:13
  47.5 4.3 %collective-permute-start.9 = (bf16[1280,768]{1,0:T(8,128)(2,1)}, bf16[1280,768]{1,0:T(8,128)(2,1)}, u32[]{:S(2)}, u32[]{:S(2)}) collective-permute-start(bf16[1280,768]{1,0:T(8,128)(2,1)} %collective-permute-done.3), channel_id=1, source_target_pairs={{4,0},{8,4},{12,8},{0,12},{5,1},{9,5},{13,9},{1,13},{6,2},{10,6},{... | collective-permute-start | bytes 5898248 | tf_op jit(solution)/shard_map/ppermute | solution.py:13
  52.7 0.7 mul.91
  54.9 0.7 mul.88
  56.0 1.6 collective-permute-start.6
  57.6 1.4 fusion.6
  59.0 34.3 %collective-permute-done.5 = s32[1,1]{1,0:T(1,128)} collective-permute-done((s32[1,1]{1,0:T(1,128)}, s32[1,1]{1,0:T(1,128)}, u32[]{:S(2)}, u32[]{:S(2)}) %collective-permute-start.5) | collective-permute-done | bytes 36 | tf_op jit(solution)/shard_map/ppermute | solution.py:13
  93.8 0.9 collective-permute-done.2
  94.7 4.3 %collective-permute-start.11 = (s32[1,1]{1,0:T(1,128)}, s32[1,1]{1,0:T(1,128)}, u32[]{:S(2)}, u32[]{:S(2)}) collective-permute-start(s32[1,1]{1,0:T(1,128)} %collective-permute-done.5), channel_id=1, source_target_pairs={{4,0},{8,4},{12,8},{0,12},{5,1},{9,5},{13,9},{1,13},{6,2},{10,6},{... | collective-permute-start | bytes 20 | tf_op jit(solution)/shard_map/ppermute | solution.py:13
  99.7 0.9 collective-permute-done.11
  101.8 3.8 %collective-permute-start.15 = (bf16[1280,768]{1,0:T(8,128)(2,1)}, bf16[1280,768]{1,0:T(8,128)(2,1)}, u32[]{:S(2)}, u32[]{:S(2)}) collective-permute-start(bf16[1280,768]{1,0:T(8,128)(2,1)} %collective-permute-done.9), channel_id=1, source_target_pairs={{4,0},{8,4},{12,8},{0,12},{5,1},{9,5},{13,9},{1,13},{6,2},{10,6},{... | collective-permute-start | bytes 5898248 | tf_op jit(solution)/shard_map/ppermute | solution.py:13
  106.2 0.9 collective-permute-start.17
  107.1 41.3 %collective-permute-done.17 = s32[1,1]{1,0:T(1,128)} collective-permute-done((s32[1,1]{1,0:T(1,128)}, s32[1,1]{1,0:T(1,128)}, u32[]{:S(2)}, u32[]{:S(2)}) %collective-permute-start.17) | collective-permute-done | bytes 36 | tf_op jit(solution)/shard_map/ppermute | solution.py:13
  151.3 0.7 mul.94
  152.0 1.4 copy.21
  153.4 1.6 collective-permute-start.7
  155.2 0.7 mul.97
  156.0 1.9 %copy.22 = bf16[160,8,3,256]{3,1,2,0:T(8,128)(2,1)} copy(bf16[160,8,3,256]{3,2,1,0:T(4,128)(2,1)S(1)} %bitcast.51) | data formatting | bytes 3932160
  157.8 4.3 %collective-permute-start.10 = (s32[1,1,15]{2,1,0:T(1,128)S(1)}, s32[1,1,15]{2,1,0:T(1,128)S(1)}, u32[]{:S(2)}, u32[]{:S(2)}) collective-permute-start(s32[1,1,15]{2,1,0:T(1,128)S(1)} %collective-permute-done.4), channel_id=1, source_target_pairs={{4,0},{8,4},{12,8},{0,12},{5,1},{9,5},{13,9},{1,13},{6,2},{10,6},{... | collective-permute-start | bytes 188 | tf_op jit(solution)/shard_map/ppermute | solution.py:13
  162.4 0.7 mul.100
  163.2 1.4 copy.23
  164.5 1.0 collective-permute-start.12
  165.8 0.7 mul.103
  166.5 1.8 copy.24
  168.6 2.0 %collective-permute-start.16 = (s32[1,1,15]{2,1,0:T(1,128)S(1)}, s32[1,1,15]{2,1,0:T(1,128)S(1)}, u32[]{:S(2)}, u32[]{:S(2)}) collective-permute-start(s32[1,1,15]{2,1,0:T(1,128)S(1)} %collective-permute-done.10), channel_id=1, source_target_pairs={{4,0},{8,4},{12,8},{0,12},{5,1},{9,5},{13,9},{1,13},{6,2},{10,6},{... | collective-permute-start | bytes 188 | tf_op jit(solution)/shard_map/ppermute | solution.py:13
  172.5 0.7 mul.109
  173.7 1.0 copy-done
  175.1 3.4 %fusion.4 = f32[512,768]{1,0:T(8,128)S(1)} fusion(bf16[1280,768]{1,0:T(8,128)(2,1)} %collective-permute-done.3, bf16[1280,768]{1,0:T(8,128)(2,1)S(1)} %bitcast.56, bf16[512,1280]{0,1:T(8,128)(2,1)} %collective-permute-done, bf16[512,1280]{0,1:T(8,128)(2,1)S(1)} %bitcast.59), kind=kOutput, calls=%fused_computation.4 | convolution fusion | flops 1008271360 | bytes 8126464 | tf_op jit(solution)/shard_map/dot_general | solution.py:36
  178.5 3.3 %fusion.2 = f32[512,768]{1,0:T(8,128)S(1)} fusion(bf16[1280,768]{1,0:T(8,128)(2,1)} %collective-permute-done.9, bf16[1280,768]{1,0:T(8,128)(2,1)S(1)} %bitcast.57, bf16[512,1280]{0,1:T(8,128)(2,1)} %collective-permute-done.6, bf16[512,1280]{0,1:T(8,128)(2,1)S(1)} %bitcast.60), kind=kOutput, calls=%fused_computation.2 | convolution fusion | flops 1008271360 | bytes 8126464 | tf_op jit(solution)/shard_map/dot_general | solution.py:36
  181.9 4.4 %add_add_fusion = f32[512,768]{1,0:T(8,128)} fusion(f32[512,768]{1,0:T(8,128)S(1)} %fusion.2, f32[512,768]{1,0:T(8,128)S(1)} %fusion.6, f32[512,768]{1,0:T(8,128)S(1)} %fusion.4, bf16[1280,768]{1,0:T(8,128)(2,1)} %collective-permute-done.15, bf16[1280,768]{1,0:T(8,128)(2,1)S(1)} %bitcast.55, bf16[512,1280]{0,1:T(8,128)(2,1)} %collective-permute-done.12, ...), kind=kOutput, calls=%fused_computation.8 | convolution fusion | flops 1009451008 | bytes 12845056 | tf_op jit(solution)/shard_map/dot_general | solution.py:36
  (71 shorter events, 11.7 us)
Async XLA Ops:
  0.0 51.7 %copy-start.8 = (s32[1,1,15]{2,1,0:T(1,128)S(1)}, s32[1,1,15]{2,1,0:T(1,128)}, u32[]{:S(2)}) copy-start(s32[1,1,15]{2,1,0:T(1,128)} %param.10) | copy-start | bytes 184
  0.0 51.8 %copy-start.7 = (s32[1,1,10]{2,1,0:T(1,128)S(1)}, s32[1,1,10]{2,1,0:T(1,128)}, u32[]{:S(2)}) copy-start(s32[1,1,10]{2,1,0:T(1,128)} %param.8) | copy-start | bytes 124
  0.0 47.4 %collective-permute-start.3 = (bf16[1280,768]{1,0:T(8,128)(2,1)}, bf16[1280,768]{1,0:T(8,128)(2,1)}, u32[]{:S(2)}, u32[]{:S(2)}) collective-permute-start(bf16[1280,768]{1,0:T(8,128)(2,1)} %param.7), channel_id=1, source_target_pairs={{4,0},{8,4},{12,8},{0,12},{5,1},{9,5},{13,9},{1,13},{6,2},{10,6},{... | collective-permute-start | bytes 5898248 | tf_op jit(solution)/shard_map/ppermute | solution.py:13
  6.7 47.3 %copy-start.4 = (bf16[512,1280]{0,1:T(8,128)(2,1)}, bf16[512,1280]{0,1:T(8,128)(2,1)S(1)}, u32[]{:S(2)}) copy-start(bf16[512,1280]{0,1:T(8,128)(2,1)S(1)} %copy.14) | copy-start | bytes 3932164
  6.7 49.3 %collective-permute-start = (bf16[512,1280]{0,1:T(8,128)(2,1)S(1)}, bf16[512,1280]{0,1:T(8,128)(2,1)}, u32[]{:S(2)}, u32[]{:S(2)}) collective-permute-start(bf16[512,1280]{0,1:T(8,128)(2,1)S(1)} %copy.14), channel_id=1, source_target_pairs={{1,0},{2,1},{3,2},{0,3},{5,4},{6,5},{7,6},{4,7},{9,8},{10,9},{11,1... | collective-permute-start | bytes 3932168 | tf_op jit(solution)/shard_map/ppermute | solution.py:13
  47.5 54.3 %collective-permute-start.9 = (bf16[1280,768]{1,0:T(8,128)(2,1)}, bf16[1280,768]{1,0:T(8,128)(2,1)}, u32[]{:S(2)}, u32[]{:S(2)}) collective-permute-start(bf16[1280,768]{1,0:T(8,128)(2,1)} %collective-permute-done.3), channel_id=1, source_target_pairs={{4,0},{8,4},{12,8},{0,12},{5,1},{9,5},{13,9},{1,13},{6,2},{10,6},{... | collective-permute-start | bytes 5898248 | tf_op jit(solution)/shard_map/ppermute | solution.py:13
  51.7 103.3 %collective-permute-start.4 = (s32[1,1,15]{2,1,0:T(1,128)S(1)}, s32[1,1,15]{2,1,0:T(1,128)S(1)}, u32[]{:S(2)}, u32[]{:S(2)}) collective-permute-start(s32[1,1,15]{2,1,0:T(1,128)S(1)} %copy-done.8), channel_id=1, source_target_pairs={{4,0},{8,4},{12,8},{0,12},{5,1},{9,5},{13,9},{1,13},{6,2},{10,6},{... | collective-permute-start | bytes 188 | tf_op jit(solution)/shard_map/ppermute | solution.py:13
  51.8 41.5 %collective-permute-start.5 = (s32[1,1]{1,0:T(1,128)}, s32[1,1]{1,0:T(1,128)}, u32[]{:S(2)}, u32[]{:S(2)}) collective-permute-start(s32[1,1]{1,0:T(1,128)} %param.11), channel_id=1, source_target_pairs={{4,0},{8,4},{12,8},{0,12},{5,1},{9,5},{13,9},{1,13},{6,2},{10,6},{... | collective-permute-start | bytes 20 | tf_op jit(solution)/shard_map/ppermute | solution.py:13
  51.8 99.2 %collective-permute-start.1 = (s32[1,1,10]{2,1,0:T(1,128)S(1)}, s32[1,1,10]{2,1,0:T(1,128)S(1)}, u32[]{:S(2)}, u32[]{:S(2)}) collective-permute-start(s32[1,1,10]{2,1,0:T(1,128)S(1)} %copy-done.7), channel_id=1, source_target_pairs={{1,0},{2,1},{3,2},{0,3},{5,4},{6,5},{7,6},{4,7},{9,8},{10,9},{11,1... | collective-permute-start | bytes 128 | tf_op jit(solution)/shard_map/ppermute | solution.py:13
  54.9 2.7 %copy-start.6 = (bf16[1280,768]{1,0:T(8,128)(2,1)S(1)}, bf16[1280,768]{1,0:T(8,128)(2,1)}, u32[]{:S(2)}) copy-start(bf16[1280,768]{1,0:T(8,128)(2,1)} %param.7) | copy-start | bytes 5898244
  55.7 2.0 %copy-start.5 = (bf16[512,1280]{0,1:T(8,128)(2,1)S(1)}, bf16[512,1280]{0,1:T(8,128)(2,1)}, u32[]{:S(2)}) copy-start(bf16[512,1280]{0,1:T(8,128)(2,1)} %copy-done.4) | copy-start | bytes 3932164
  56.0 108.5 %collective-permute-start.6 = (bf16[512,1280]{0,1:T(8,128)(2,1)}, bf16[512,1280]{0,1:T(8,128)(2,1)}, u32[]{:S(2)}, u32[]{:S(2)}) collective-permute-start(bf16[512,1280]{0,1:T(8,128)(2,1)} %collective-permute-done), channel_id=1, source_target_pairs={{1,0},{2,1},{3,2},{0,3},{5,4},{6,5},{7,6},{4,7},{9,8},{10,9},{11,1... | collective-permute-start | bytes 3932168 | tf_op jit(solution)/shard_map/ppermute | solution.py:13
  93.3 1.4 collective-permute-start.2
  94.7 5.9 %collective-permute-start.11 = (s32[1,1]{1,0:T(1,128)}, s32[1,1]{1,0:T(1,128)}, u32[]{:S(2)}, u32[]{:S(2)}) collective-permute-start(s32[1,1]{1,0:T(1,128)} %collective-permute-done.5), channel_id=1, source_target_pairs={{4,0},{8,4},{12,8},{0,12},{5,1},{9,5},{13,9},{1,13},{6,2},{10,6},{... | collective-permute-start | bytes 20 | tf_op jit(solution)/shard_map/ppermute | solution.py:13
  100.6 5.0 %collective-permute-start.8 = (s32[1,1]{1,0:T(1,128)}, s32[1,1]{1,0:T(1,128)}, u32[]{:S(2)}, u32[]{:S(2)}) collective-permute-start(s32[1,1]{1,0:T(1,128)} %collective-permute-done.2), channel_id=1, source_target_pairs={{1,0},{2,1},{3,2},{0,3},{5,4},{6,5},{7,6},{4,7},{9,8},{10,9},{11,1... | collective-permute-start | bytes 20 | tf_op jit(solution)/shard_map/ppermute | solution.py:13
  101.8 80.1 %collective-permute-start.15 = (bf16[1280,768]{1,0:T(8,128)(2,1)}, bf16[1280,768]{1,0:T(8,128)(2,1)}, u32[]{:S(2)}, u32[]{:S(2)}) collective-permute-start(bf16[1280,768]{1,0:T(8,128)(2,1)} %collective-permute-done.9), channel_id=1, source_target_pairs={{4,0},{8,4},{12,8},{0,12},{5,1},{9,5},{13,9},{1,13},{6,2},{10,6},{... | collective-permute-start | bytes 5898248 | tf_op jit(solution)/shard_map/ppermute | solution.py:13
  106.2 42.2 %collective-permute-start.17 = (s32[1,1]{1,0:T(1,128)}, s32[1,1]{1,0:T(1,128)}, u32[]{:S(2)}, u32[]{:S(2)}) collective-permute-start(s32[1,1]{1,0:T(1,128)} %collective-permute-done.11), channel_id=1, source_target_pairs={{4,0},{8,4},{12,8},{0,12},{5,1},{9,5},{13,9},{1,13},{6,2},{10,6},{... | collective-permute-start | bytes 20 | tf_op jit(solution)/shard_map/ppermute | solution.py:13
  148.4 2.0 %collective-permute-start.14 = (s32[1,1]{1,0:T(1,128)}, s32[1,1]{1,0:T(1,128)}, u32[]{:S(2)}, u32[]{:S(2)}) collective-permute-start(s32[1,1]{1,0:T(1,128)} %collective-permute-done.8), channel_id=1, source_target_pairs={{1,0},{2,1},{3,2},{0,3},{5,4},{6,5},{7,6},{4,7},{9,8},{10,9},{11,1... | collective-permute-start | bytes 20 | tf_op jit(solution)/shard_map/ppermute | solution.py:13
  153.4 8.7 %collective-permute-start.7 = (s32[1,1,10]{2,1,0:T(1,128)S(1)}, s32[1,1,10]{2,1,0:T(1,128)S(1)}, u32[]{:S(2)}, u32[]{:S(2)}) collective-permute-start(s32[1,1,10]{2,1,0:T(1,128)S(1)} %collective-permute-done.1), channel_id=1, source_target_pairs={{1,0},{2,1},{3,2},{0,3},{5,4},{6,5},{7,6},{4,7},{9,8},{10,9},{11,1... | collective-permute-start | bytes 128 | tf_op jit(solution)/shard_map/ppermute | solution.py:13
  157.8 7.7 %collective-permute-start.10 = (s32[1,1,15]{2,1,0:T(1,128)S(1)}, s32[1,1,15]{2,1,0:T(1,128)S(1)}, u32[]{:S(2)}, u32[]{:S(2)}) collective-permute-start(s32[1,1,15]{2,1,0:T(1,128)S(1)} %collective-permute-done.4), channel_id=1, source_target_pairs={{4,0},{8,4},{12,8},{0,12},{5,1},{9,5},{13,9},{1,13},{6,2},{10,6},{... | collective-permute-start | bytes 188 | tf_op jit(solution)/shard_map/ppermute | solution.py:13
  164.5 3.8 %collective-permute-start.13 = (s32[1,1,10]{2,1,0:T(1,128)S(1)}, s32[1,1,10]{2,1,0:T(1,128)S(1)}, u32[]{:S(2)}, u32[]{:S(2)}) collective-permute-start(s32[1,1,10]{2,1,0:T(1,128)S(1)} %collective-permute-done.7), channel_id=1, source_target_pairs={{1,0},{2,1},{3,2},{0,3},{5,4},{6,5},{7,6},{4,7},{9,8},{10,9},{11,1... | collective-permute-start | bytes 128 | tf_op jit(solution)/shard_map/ppermute | solution.py:13
  164.5 17.3 %collective-permute-start.12 = (bf16[512,1280]{0,1:T(8,128)(2,1)}, bf16[512,1280]{0,1:T(8,128)(2,1)}, u32[]{:S(2)}, u32[]{:S(2)}) collective-permute-start(bf16[512,1280]{0,1:T(8,128)(2,1)} %collective-permute-done.6), channel_id=1, source_target_pairs={{1,0},{2,1},{3,2},{0,3},{5,4},{6,5},{7,6},{4,7},{9,8},{10,9},{11,1... | collective-permute-start | bytes 3932168 | tf_op jit(solution)/shard_map/ppermute | solution.py:13
  168.6 3.7 %collective-permute-start.16 = (s32[1,1,15]{2,1,0:T(1,128)S(1)}, s32[1,1,15]{2,1,0:T(1,128)S(1)}, u32[]{:S(2)}, u32[]{:S(2)}) collective-permute-start(s32[1,1,15]{2,1,0:T(1,128)S(1)} %collective-permute-done.10), channel_id=1, source_target_pairs={{4,0},{8,4},{12,8},{0,12},{5,1},{9,5},{13,9},{1,13},{6,2},{10,6},{... | collective-permute-start | bytes 188 | tf_op jit(solution)/shard_map/ppermute | solution.py:13
  173.2 1.5 copy-start
  173.2 1.9 %copy-start.2 = (bf16[160,8,2,256]{3,1,2,0:T(8,128)(2,1)S(1)}, bf16[160,8,2,256]{3,1,2,0:T(8,128)(2,1)}, u32[]{:S(2)}) copy-start(bf16[160,8,2,256]{3,1,2,0:T(8,128)(2,1)} %copy.21) | copy-start | bytes 3932164
  175.1 3.4 %copy-start.1 = (bf16[160,8,3,256]{3,1,2,0:T(8,128)(2,1)S(1)}, bf16[160,8,3,256]{3,1,2,0:T(8,128)(2,1)}, u32[]{:S(2)}) copy-start(bf16[160,8,3,256]{3,1,2,0:T(8,128)(2,1)} %copy.24) | copy-start | bytes 5898244
  175.1 3.4 %copy-start.3 = (bf16[160,8,2,256]{3,1,2,0:T(8,128)(2,1)S(1)}, bf16[160,8,2,256]{3,1,2,0:T(8,128)(2,1)}, u32[]{:S(2)}) copy-start(bf16[160,8,2,256]{3,1,2,0:T(8,128)(2,1)} %copy.23) | copy-start | bytes 3932164
where the time goes:
time: 187 us; the launch traced here: 186 us
  waiting for transfers between devices  119 us (64%)
  starting transfers between devices  30.9 us (17%)
  local copies, waits for them, and re-layouts  18.1 us (10%)
  matrix products  12.5 us (7%)
  other arithmetic  4.41 us (2%)
    ppermute x18, waiting for transfers between devices, passed_along(): return lax.ppermute(block, axis, route)  119 us
    ppermute x18, starting transfers between devices, passed_along(): return lax.ppermute(block, axis, route)  30.9 us
    dot_general x4, matrix products, on_device(): jnp.dot(masked(held_left[0], held_left[1], held_left[2], left_rows, inner...  12.5 us
    unnamed x27, local copies, waits for them, and re-layouts  11 us
    mul x8, local copies, waits for them, and re-layouts, masked(): tile.reshape(block_rows, BW, block_cols, BW)  5.96 us
  transfers between devices with their start and end apart: 18, of which 7 were waited for; matrix products, arithmetic and copies ran while one was open for 16% of the time, Pallas kernels for 0%

commit v1 on v0

--- a/solution.py
+++ b/solution.py
@@ -1,10 +1,16 @@
+import functools
+
 import jax
 import jax.numpy as jnp
 from jax import lax
+from jax.experimental import pallas as pl
+from jax.experimental.pallas import tpu as pltpu
 from jax.sharding import PartitionSpec as P
 
 BW = 256
+CAP = 4
 STEPS = 4
+MESH = pl.DeviceIdType.MESH
 
 
 def passed_along(block, axis, distance):
@@ -25,7 +31,7 @@
     return shaped.reshape(tile.shape)
 
 
-def on_device(left_tiles, right_tiles, left_blocks, left_count, right_blocks, right_count):
+def shifted_steps(left_tiles, right_tiles, left_blocks, left_count, right_blocks, right_count):
     left_rows = left_tiles.shape[0] // BW
     inner_blocks = left_tiles.shape[1] // BW
     right_cols = right_tiles.shape[1] // BW
@@ -39,9 +45,292 @@
             preferred_element_type=jnp.float32,
         )
         if step + 1 < STEPS:
-            held_left = passed_along((held_left[0], held_left[1], held_left[2]), "col", -1)
-            held_right = passed_along((held_right[0], held_right[1], held_right[2]), "row", -1)
+            held_left = passed_along(held_left, "col", -1)
+            held_right = passed_along(held_right, "row", -1)
     return total
+
+
+K_AT, C_AT = 16, 20
+
+
+def kernel(
+    left_ref, right_ref, left_blocks, left_count, right_blocks, right_count, out_ref,
+    left_full, right_full, left_own, left_held, right_held, total, note,
+    notes_row, notes_col, read_row, read_col,
+    right_load, left_load, out_sem, note_sem, right_send, right_recv, left_send, left_recv, notes_send, notes_recv,
+):
+    z, j = lax.axis_index("row"), lax.axis_index("col")
+    kb = left_ref.shape[1] // BW
+    rb = left_ref.shape[0] // BW
+    cb = right_ref.shape[1] // BW
+    sibling = j + 1 - 2 * lax.rem(j, 2)
+    partner = lax.rem(j + 2, 4)
+    far = lax.rem(sibling + 2, 4)
+
+    right_loads = [
+        pltpu.make_async_copy(
+            right_ref.at[pl.ds(b // cb * BW, BW), pl.ds(b % cb * BW, BW)], right_full.at[b], right_load.at[b]
+        )
+        for b in range(kb * cb)
+    ]
+    left_loads = [
+        pltpu.make_async_copy(
+            left_ref.at[pl.ds(b // kb * BW, BW), pl.ds(b % kb * BW, BW)], left_full.at[b], left_load.at[b]
+        )
+        for b in range(rb * kb)
+    ]
+    for load in right_loads + left_loads:
+        load.start()
+
+    barrier = pltpu.get_barrier_semaphore()
+    for d in range(1, 4):
+        pl.semaphore_signal(barrier, inc=1, device_id={"row": lax.rem(z + d, 4)}, device_id_type=MESH)
+        pl.semaphore_signal(barrier, inc=1, device_id={"col": lax.rem(j + d, 4)}, device_id_type=MESH)
+
+    lane = lax.broadcasted_iota(jnp.int32, note.shape, 1)
+    told = jnp.full(note.shape, CAP, jnp.int32)
+    for n in range(CAP):
+        told = jnp.where(lane == jnp.where(n < left_count[0, 0], left_blocks[0, 0, n], -1), n, told)
+        told = jnp.where(lane == K_AT + n, lax.div(right_blocks[0, 0, n], cb), told)
+        column = jnp.where(n < right_count[0, 0], lax.rem(right_blocks[0, 0, n], cb), cb)
+        told = jnp.where(lane == C_AT + n, column, told)
+    note[...] = told
+    notes_row[z] = told
+    notes_col[j] = told
+
+    empty = jnp.zeros((BW, BW), jnp.bfloat16)
+    left_own[CAP] = empty
+    for t in range(4):
+        left_held[t, CAP] = empty
+
+    def send_right(t, b, up):
+        return pltpu.make_async_remote_copy(
+            src_ref=right_held.at[t, b], dst_ref=right_held.at[t, b],
+            send_sem=right_send.at[up, t, b], recv_sem=right_recv.at[t, b],
+            device_id={"row": lax.rem(z + (1 if up else 3), 4)}, device_id_type=MESH,
+        )
+
+    def send_left(b, to):
+        return pltpu.make_async_remote_copy(
+            src_ref=left_own.at[b], dst_ref=left_held.at[j, b],
+            send_sem=left_send.at[0 if to is partner else 1, b], recv_sem=left_recv.at[j, b],
+            device_id={"col": to}, device_id_type=MESH,
+        )
+
+    def pass_left(b):
+        return pltpu.make_async_remote_copy(
+            src_ref=left_held.at[partner, b], dst_ref=left_held.at[partner, b],
+            send_sem=left_send.at[2, b], recv_sem=left_recv.at[partner, b],
+            device_id={"col": sibling}, device_id_type=MESH,
+        )
+
+    def got_left(t, b):
+        pltpu.make_async_remote_copy(
+            src_ref=left_held.at[t, b], dst_ref=left_held.at[t, b],
+            send_sem=left_send.at[0, b], recv_sem=left_recv.at[t, b],
+            device_id={"col": sibling}, device_id_type=MESH,
+        ).wait_recv()
+
+    def send_note(d, axis):
+        own = z if axis == 0 else j
+        held = notes_row if axis == 0 else notes_col
+        return pltpu.make_async_remote_copy(
+            src_ref=note, dst_ref=held.at[own],
+            send_sem=notes_send.at[axis, d], recv_sem=notes_recv.at[axis, own],
+            device_id={"row" if axis == 0 else "col": lax.rem(own + d, 4)}, device_id_type=MESH,
+        )
+
+    def got_note(d, axis):
+        own = z if axis == 0 else j
+        held = notes_row if axis == 0 else notes_col
+        t = lax.rem(own + d, 4)
+        pltpu.make_async_remote_copy(
+            src_ref=note, dst_ref=held.at[t],
+            send_sem=notes_send.at[axis, d], recv_sem=notes_recv.at[axis, t],
+            device_id={"row" if axis == 0 else "col": t}, device_id_type=MESH,
+        ).wait_recv()
+
+    pl.semaphore_wait(barrier, 6)
+
+    for load in right_loads:
+        load.wait()
+    for n in range(CAP):
+        right_held[z, n] = right_full[right_blocks[0, 0, n]]
+
+        @pl.when(z < 3)
+        def _():
+            send_right(z, n, 1).start()
+
+        @pl.when(z > 0)
+        def _():
+            send_right(z, n, 0).start()
+
+    for load in left_loads:
+        load.wait()
+    for n in range(CAP):
+        left_own[n] = left_full[left_blocks[0, 0, n]]
+        send_left(n, partner).start()
+        send_left(n, sibling).start()
+
+    for axis in range(2):
+        for d in range(1, 4):
+            send_note(d, axis).start()
+
+    total[...] = jnp.zeros_like(total)
+
+    for axis in range(2):
+        for d in range(1, 4):
+            got_note(d, axis)
+    reads = (
+        pltpu.make_async_copy(notes_row, read_row, note_sem.at[0]),
+        pltpu.make_async_copy(notes_col, read_col, note_sem.at[1]),
+    )
+    for read in reads:
+        read.start()
+    for read in reads:
+        read.wait()
+
+    def add(t, b, own):
+        k, c = read_row[t, 0, K_AT + b], read_row[t, 0, C_AT + b]
+        l = j if own else lax.rem(j + t - z + 4, 4)
+        block = right_held[t, b]
+        for r in range(rb):
+            slot = read_col[l, 0, r * kb + k]
+            met = left_own[slot] if own else left_held[l, slot]
+            product = jnp.dot(met, block, preferred_element_type=jnp.float32)
+            for at in range(cb):
+                place = (pl.ds(r * BW, BW), pl.ds(at * BW, BW))
+                total[place] += jnp.where(c == at, product, 0.0)
+
+    def take_right(d, b):
+        @pl.when(z >= d)
+        def _():
+            send_right(z - d, b, 0).wait_recv()
+            if d < 3:
+
+                @pl.when(z < 3)
+                def _():
+                    send_right(z - d, b, 1).start()
+
+        @pl.when(z + d < 4)
+        def _():
+            send_right(z + d, b, 0).wait_recv()
+            if d < 3:
+
+                @pl.when(z > 0)
+                def _():
+                    send_right(z + d, b, 0).start()
+
+    def first(b, carry):
+        take_right(1, b)
+        got_left(partner, b)
+        pass_left(b).start()
+        add(z, b, True)
+        return carry
+
+    lax.fori_loop(0, CAP, first, 0)
+
+    def rest_of_left(b, carry):
+        got_left(sibling, b)
+        got_left(far, b)
+        return carry
+
+    lax.fori_loop(0, CAP, rest_of_left, 0)
+
+    def second(b, carry):
+        take_right(2, b)
+
+        @pl.when(z > 0)
+        def _():
+            add(z - 1, b, False)
+
+        @pl.when(z < 3)
+        def _():
+            add(z + 1, b, False)
+
+        return carry
+
+    lax.fori_loop(0, CAP, second, 0)
+
+    def third(b, carry):
+        add(lax.rem(z + 2, 4), b, False)
+        take_right(3, b)
+
+        @pl.when((z == 0) | (z == 3))
+        def _():
+            add(3 - z, b, False)
+
+        return carry
+
+    lax.fori_loop(0, CAP, third, 0)
+
+    out = pltpu.make_async_copy(total, out_ref, out_sem.at[0])
+    out.start()
+
+    def sent(b, carry):
+        send_left(b, partner).wait_send()
+        send_left(b, sibling).wait_send()
+        pass_left(b).wait_send()
+        for d in range(3):
+
+            @pl.when((z >= d) & (z < 3))
+            def _():
+                send_right(z - d, b, 1).wait_send()
+
+            @pl.when((z + d < 4) & (z > 0))
+            def _():
+                send_right(z + d, b, 0).wait_send()
+
+        return carry
+
+    lax.fori_loop(0, CAP, sent, 0)
+    for axis in range(2):
+        for d in range(1, 4):
+            send_note(d, axis).wait_send()
+    out.wait()
+
+
+def packed_lines(left_tiles, right_tiles, left_blocks, left_count, right_blocks, right_count):
+    rows, cols = left_tiles.shape[0], right_tiles.shape[1]
+    left_total, right_total = left_tiles.size // BW**2, right_tiles.size // BW**2
+    any_space = pl.BlockSpec(memory_space=pl.ANY)
+    scalars = pl.BlockSpec(memory_space=pltpu.SMEM)
+    dma = pltpu.SemaphoreType.DMA
+    return pl.pallas_call(
+        kernel,
+        out_shape=jax.ShapeDtypeStruct((rows, cols), jnp.float32),
+        in_specs=[any_space] * 2 + [scalars] * 4,
+        out_specs=any_space,
+        scratch_shapes=[
+            pltpu.VMEM((left_total, BW, BW), jnp.bfloat16),
+            pltpu.VMEM((right_total, BW, BW), jnp.bfloat16),
+            pltpu.VMEM((CAP + 1, BW, BW), jnp.bfloat16),
+            pltpu.VMEM((4, CAP + 1, BW, BW), jnp.bfloat16),
+            pltpu.VMEM((4, CAP, BW, BW), jnp.bfloat16),
+            pltpu.VMEM((rows, cols), jnp.float32),
+            pltpu.VMEM((8, 128), jnp.int32),
+            pltpu.VMEM((4, 8, 128), jnp.int32),
+            pltpu.VMEM((4, 8, 128), jnp.int32),
+            pltpu.SMEM((4, 8, 128), jnp.int32),
+            pltpu.SMEM((4, 8, 128), jnp.int32),
+            dma((right_total,)),
+            dma((left_total,)),
+            dma((1,)),
+            dma((2,)),
+            dma((2, 4, CAP)),
+            dma((4, CAP)),
+            dma((3, CAP)),
+            dma((4, CAP)),
+            dma((2, 4)),
+            dma((2, 4)),
+        ],
+        compiler_params=pltpu.CompilerParams(
+            collective_id=0, has_side_effects=True, vmem_limit_bytes=56 * 1024 * 1024
+        ),
+        cost_estimate=pl.CostEstimate(
+            flops=2 * STEPS * 2 * CAP * BW**3, bytes_accessed=5 * 1024 * 1024, transcendentals=0
+        ),
+    )(left_tiles, right_tiles, left_blocks, left_count, right_blocks, right_count)
 
 
 def solution(mesh):
@@ -53,8 +342,9 @@
         P(("groups", "row"), "col", None),
         P(("groups", "row"), "col"),
     )
+    grid = mesh.shape["row"] == 4 and mesh.shape["col"] == 4
     return jax.shard_map(
-        on_device,
+        packed_lines if grid else shifted_steps,
         mesh=mesh,
         in_specs=placed,
         out_specs=P(("groups", "row"), "col"),

time: 187 us -> 50.9 us (0.27)
  waiting for transfers between devices: 119 us -> 0 us
  Pallas kernels: 0 us -> 46.8 us
  starting transfers between devices: 30.9 us -> 0 us
  local copies, waits for them, and re-layouts: 18.1 us -> 2.65 us
  matrix products: 12.5 us -> 0 us
  other arithmetic: 4.41 us -> 0 us
    ppermute x18 -> x0, waiting for transfers between devices: 119 us -> none  [passed_along(): return lax.ppermute(block, axis, route)]
    pallas_call x0 -> x1, Pallas kernels: none -> 46.8 us  [packed_lines(): pl.pallas_call(kernel, out_shape=jax.ShapeDtypeStruct((rows, cols), jnp.f...]
    ppermute x18 -> x0, starting transfers between devices: 30.9 us -> none  [passed_along(): return lax.ppermute(block, axis, route)]
    dot_general x4 -> x0, matrix products: 12.5 us -> none  [on_device(): jnp.dot(masked(held_left[0], held_left[1], held_left[2], left_rows, inner...]
    unnamed x27 -> x1, local copies, waits for them, and re-layouts: 11 us -> 2.65 us
    mul x8 -> x0, local copies, waits for them, and re-layouts: 5.96 us -> none  [masked(): tile.reshape(block_rows, BW, block_cols, BW)]
    lt x8 -> x0, other arithmetic: 3.67 us -> none  [masked(): slot_index[:, None] < occupied[0, 0]]
  transfers between devices with their start and end apart: 18 -> 0, of which waited for: 7 -> 0; matrix products, arithmetic and copies ran while one was open for 16% -> 0% of each run, Pallas kernels for 0% -> 0%
where the time goes in v1:
time: 50.9 us; the launch traced here: 50.7 us
  Pallas kernels  46.8 us (92%)
  local copies, waits for them, and re-layouts  2.65 us (5%)
  between operations  1.3 us (3%)
    pallas_call x1, Pallas kernels, packed_lines(): pl.pallas_call(kernel, out_shape=jax.ShapeDtypeStruct((rows, cols), jnp.f...  46.8 us
    unnamed x1, local copies, waits for them, and re-layouts  2.65 us

profile of v1, /device:TPU:0, one launch (start us, length us, event | category | flops | bytes accessed | tf_op | source)
XLA Modules:
  0.0 50.7 jit_solution(5908551648634582362)
XLA Ops:
  1.3 46.8 %shard_map.64 = f32[512,768]{1,0:T(8,128)} custom-call(bf16[512,1280]{1,0:T(8,128)(2,1)} %left_ref.1, bf16[1280,768]{1,0:T(8,128)(2,1)} %right_ref.1, s32[1,1,10]{2,1,0:T(1,128)} %left_blocks.1, s32[1,1]{1,0:T(1,128)S(6)} %copy.8.left_count, s32[1,1,15]{2,1,0:T(1,128)} %right_blocks.1, s32[1,1]{1,0:T(1,128)S(6)} %copy.9.right_count), custom_call_target="tpu_custom_call" | custom-call | flops 1073741824 | bytes 5242880 | tf_op jit(solution)/shard_map/pallas_call | solution.py:299
  48.1 2.7 %copy.10 = f32[512,768]{1,0:T(8,128)} copy(f32[512,768]{1,0:T(8,128)} %shard_map.64) | data formatting | bytes 3145728

commit v2 on v1

--- a/solution.py
+++ b/solution.py
@@ -9,6 +9,7 @@
 
 BW = 256
 CAP = 4
+AHEAD = 4
 STEPS = 4
 MESH = pl.DeviceIdType.MESH
 
@@ -54,10 +55,10 @@
 
 
 def kernel(
-    left_ref, right_ref, left_blocks, left_count, right_blocks, right_count, out_ref,
-    left_full, right_full, left_own, left_held, right_held, total, note,
-    notes_row, notes_col, read_row, read_col,
-    right_load, left_load, out_sem, note_sem, right_send, right_recv, left_send, left_recv, notes_send, notes_recv,
+    left_ref, right_ref, left_blocks, left_count, right_blocks, right_count, total,
+    left_full, right_full, left_own, left_held, right_held, note,
+    notes_row, notes_col, read_own, read_row, read_col,
+    right_load, left_load, note_sem, right_send, right_recv, left_send, left_recv, notes_send, notes_recv,
 ):
     z, j = lax.axis_index("row"), lax.axis_index("col")
     kb = left_ref.shape[1] // BW
@@ -97,6 +98,8 @@
     note[...] = told
     notes_row[z] = told
     notes_col[j] = told
+    own_read = pltpu.make_async_copy(note, read_own, note_sem.at[2])
+    own_read.start()
 
     empty = jnp.zeros((BW, BW), jnp.bfloat16)
     left_own[CAP] = empty
@@ -109,6 +112,15 @@
             send_sem=right_send.at[up, t, b], recv_sem=right_recv.at[t, b],
             device_id={"row": lax.rem(z + (1 if up else 3), 4)}, device_id_type=MESH,
         )
+
+    def send_own(b):
+        @pl.when(z < 3)
+        def _():
+            send_right(z, b, 1).start()
+
+        @pl.when(z > 0)
+        def _():
+            send_right(z, b, 0).start()
 
     def send_left(b, to):
         return pltpu.make_async_remote_copy(
@@ -151,19 +163,16 @@
         ).wait_recv()
 
     pl.semaphore_wait(barrier, 6)
+    for axis in range(2):
+        for d in range(1, 4):
+            send_note(d, axis).start()
 
     for load in right_loads:
         load.wait()
     for n in range(CAP):
         right_held[z, n] = right_full[right_blocks[0, 0, n]]
-
-        @pl.when(z < 3)
-        def _():
-            send_right(z, n, 1).start()
-
-        @pl.when(z > 0)
-        def _():
-            send_right(z, n, 0).start()
+        if n < AHEAD:
+            send_own(n)
 
     for load in left_loads:
         load.wait()
@@ -172,12 +181,62 @@
         send_left(n, partner).start()
         send_left(n, sibling).start()
 
-    for axis in range(2):
-        for d in range(1, 4):
-            send_note(d, axis).start()
-
     total[...] = jnp.zeros_like(total)
 
+    own_read.wait()
+
+    def add(t, b, own):
+        l = lax.rem(j + t - z + 4, 4)
+        k = read_own[0, K_AT + b] if own else read_row[t, 0, K_AT + b]
+        c = read_own[0, C_AT + b] if own else read_row[t, 0, C_AT + b]
+        block = right_held[t, b]
+        for r in range(rb):
+            slot = read_own[0, r * kb + k] if own else read_col[l, 0, r * kb + k]
+            met = left_own[slot] if own else left_held[l, slot]
+            product = jnp.dot(met, block, preferred_element_type=jnp.float32)
+            for at in range(cb):
+                place = (pl.ds(r * BW, BW), pl.ds(at * BW, BW))
+                total[place] += jnp.where(c == at, product, 0.0)
+
+    def take_right(d, b):
+        @pl.when(z >= d)
+        def _():
+            send_right(z - d, b, 0).wait_recv()
+            if d < 3:
+
+                @pl.when(z < 3)
+                def _():
+                    send_right(z - d, b, 1).start()
+
+        @pl.when(z + d < 4)
+        def _():
+            send_right(z + d, b, 0).wait_recv()
+            if d < 3:
+
+                @pl.when(z > 0)
+                def _():
+                    send_right(z + d, b, 0).start()
+
+    def first(b, carry):
+        take_right(1, b)
+
+        @pl.when(b + AHEAD < CAP)
+        def _():
+            send_own(b + AHEAD)
+
+        got_left(partner, b)
+        pass_left(b).start()
+        add(z, b, True)
+        return carry
+
+    lax.fori_loop(0, CAP, first, 0)
+
+    def rest_of_left(b, carry):
+        got_left(sibling, b)
+        got_left(far, b)
+        return carry
+
+    lax.fori_loop(0, CAP, rest_of_left, 0)
     for axis in range(2):
         for d in range(1, 4):
             got_note(d, axis)
@@ -190,53 +249,6 @@
     for read in reads:
         read.wait()
 
-    def add(t, b, own):
-        k, c = read_row[t, 0, K_AT + b], read_row[t, 0, C_AT + b]
-        l = j if own else lax.rem(j + t - z + 4, 4)
-        block = right_held[t, b]
-        for r in range(rb):
-            slot = read_col[l, 0, r * kb + k]
-            met = left_own[slot] if own else left_held[l, slot]
-            product = jnp.dot(met, block, preferred_element_type=jnp.float32)
-            for at in range(cb):
-                place = (pl.ds(r * BW, BW), pl.ds(at * BW, BW))
-                total[place] += jnp.where(c == at, product, 0.0)
-
-    def take_right(d, b):
-        @pl.when(z >= d)
-        def _():
-            send_right(z - d, b, 0).wait_recv()
-            if d < 3:
-
-                @pl.when(z < 3)
-                def _():
-                    send_right(z - d, b, 1).start()
-
-        @pl.when(z + d < 4)
-        def _():
-            send_right(z + d, b, 0).wait_recv()
-            if d < 3:
-
-                @pl.when(z > 0)
-                def _():
-                    send_right(z + d, b, 0).start()
-
-    def first(b, carry):
-        take_right(1, b)
-        got_left(partner, b)
-        pass_left(b).start()
-        add(z, b, True)
-        return carry
-
-    lax.fori_loop(0, CAP, first, 0)
-
-    def rest_of_left(b, carry):
-        got_left(sibling, b)
-        got_left(far, b)
-        return carry
-
-    lax.fori_loop(0, CAP, rest_of_left, 0)
-
     def second(b, carry):
         take_right(2, b)
 
@@ -263,9 +275,6 @@
         return carry
 
     lax.fori_loop(0, CAP, third, 0)
-
-    out = pltpu.make_async_copy(total, out_ref, out_sem.at[0])
-    out.start()
 
     def sent(b, carry):
         send_left(b, partner).wait_send()
@@ -287,7 +296,6 @@
     for axis in range(2):
         for d in range(1, 4):
             send_note(d, axis).wait_send()
-    out.wait()
 
 
 def packed_lines(left_tiles, right_tiles, left_blocks, left_count, right_blocks, right_count):
@@ -298,25 +306,24 @@
     dma = pltpu.SemaphoreType.DMA
     return pl.pallas_call(
         kernel,
-        out_shape=jax.ShapeDtypeStruct((rows, cols), jnp.float32),
+        out_shape=pltpu.VMEM((rows, cols), jnp.float32),
         in_specs=[any_space] * 2 + [scalars] * 4,
-        out_specs=any_space,
+        out_specs=pl.BlockSpec(memory_space=pltpu.VMEM),
         scratch_shapes=[
             pltpu.VMEM((left_total, BW, BW), jnp.bfloat16),
             pltpu.VMEM((right_total, BW, BW), jnp.bfloat16),
             pltpu.VMEM((CAP + 1, BW, BW), jnp.bfloat16),
             pltpu.VMEM((4, CAP + 1, BW, BW), jnp.bfloat16),
             pltpu.VMEM((4, CAP, BW, BW), jnp.bfloat16),
-            pltpu.VMEM((rows, cols), jnp.float32),
             pltpu.VMEM((8, 128), jnp.int32),
             pltpu.VMEM((4, 8, 128), jnp.int32),
             pltpu.VMEM((4, 8, 128), jnp.int32),
+            pltpu.SMEM((8, 128), jnp.int32),
             pltpu.SMEM((4, 8, 128), jnp.int32),
             pltpu.SMEM((4, 8, 128), jnp.int32),
             dma((right_total,)),
             dma((left_total,)),
-            dma((1,)),
-            dma((2,)),
+            dma((3,)),
             dma((2, 4, CAP)),
             dma((4, CAP)),
             dma((3, CAP)),

time: 50.9 us -> 44.8 us (0.88)
  Pallas kernels: 46.8 us -> 42.2 us
  local copies, waits for them, and re-layouts: 2.65 us -> 1.15 us
    pallas_call x1, Pallas kernels: 46.8 us -> 42.2 us  [packed_lines(): pl.pallas_call(kernel, out_shape=pltpu.VMEM((rows, cols), jnp.float32), i...]
    unnamed x1, local copies, waits for them, and re-layouts: 2.65 us -> 1.15 us
where the time goes in v2:
time: 44.8 us; the launch traced here: 44.7 us
  Pallas kernels  42.2 us (94%)
  between operations  1.3 us (3%)
  local copies, waits for them, and re-layouts  1.15 us (3%)
    pallas_call x1, Pallas kernels, packed_lines(): pl.pallas_call(kernel, out_shape=pltpu.VMEM((rows, cols), jnp.float32), i...  42.2 us
    unnamed x1, local copies, waits for them, and re-layouts  1.15 us

profile of v2, /device:TPU:0, one launch (start us, length us, event | category | flops | bytes accessed | tf_op | source)
XLA Modules:
  0.0 44.7 jit_solution(4178279435611989574)
XLA Ops:
  1.3 42.2 %shard_map.64 = f32[512,768]{1,0:T(8,128)S(1)} custom-call(bf16[512,1280]{1,0:T(8,128)(2,1)} %left_ref.1, bf16[1280,768]{1,0:T(8,128)(2,1)} %right_ref.1, s32[1,1,10]{2,1,0:T(1,128)} %left_blocks.1, s32[1,1]{1,0:T(1,128)S(6)} %copy.9.left_count, s32[1,1,15]{2,1,0:T(1,128)} %right_blocks.1, s32[1,1]{1,0:T(1,128)S(6)} %copy.10.right_count), custom_call_target="tpu_custom_call" | custom-call | flops 1073741824 | bytes 5242880 | tf_op jit(solution)/shard_map/pallas_call | solution.py:307
  43.5 1.1 %copy.8 = f32[512,768]{1,0:T(8,128)} copy(f32[512,768]{1,0:T(8,128)S(1)} %shard_map.64) | data formatting | bytes 3145728

commit v3 on v2

--- a/solution.py
+++ b/solution.py
@@ -9,7 +9,6 @@
 
 BW = 256
 CAP = 4
-AHEAD = 4
 STEPS = 4
 MESH = pl.DeviceIdType.MESH
 
@@ -58,7 +57,7 @@
     left_ref, right_ref, left_blocks, left_count, right_blocks, right_count, total,
     left_full, right_full, left_own, left_held, right_held, note,
     notes_row, notes_col, read_own, read_row, read_col,
-    right_load, left_load, note_sem, right_send, right_recv, left_send, left_recv, notes_send, notes_recv,
+    right_load, left_load, note_sem, right_send, right_recv, left_send, left_recv, row_notes_send, row_notes_recv, notes_send, notes_recv,
 ):
     z, j = lax.axis_index("row"), lax.axis_index("col")
     kb = left_ref.shape[1] // BW
@@ -85,7 +84,6 @@
 
     barrier = pltpu.get_barrier_semaphore()
     for d in range(1, 4):
-        pl.semaphore_signal(barrier, inc=1, device_id={"row": lax.rem(z + d, 4)}, device_id_type=MESH)
         pl.semaphore_signal(barrier, inc=1, device_id={"col": lax.rem(j + d, 4)}, device_id_type=MESH)
 
     lane = lax.broadcasted_iota(jnp.int32, note.shape, 1)
@@ -113,15 +111,6 @@
             device_id={"row": lax.rem(z + (1 if up else 3), 4)}, device_id_type=MESH,
         )
 
-    def send_own(b):
-        @pl.when(z < 3)
-        def _():
-            send_right(z, b, 1).start()
-
-        @pl.when(z > 0)
-        def _():
-            send_right(z, b, 0).start()
-
     def send_left(b, to):
         return pltpu.make_async_remote_copy(
             src_ref=left_own.at[b], dst_ref=left_held.at[j, b],
@@ -143,36 +132,57 @@
             device_id={"col": sibling}, device_id_type=MESH,
         ).wait_recv()
 
-    def send_note(d, axis):
-        own = z if axis == 0 else j
-        held = notes_row if axis == 0 else notes_col
-        return pltpu.make_async_remote_copy(
-            src_ref=note, dst_ref=held.at[own],
-            send_sem=notes_send.at[axis, d], recv_sem=notes_recv.at[axis, own],
-            device_id={"row" if axis == 0 else "col": lax.rem(own + d, 4)}, device_id_type=MESH,
-        )
-
-    def got_note(d, axis):
-        own = z if axis == 0 else j
-        held = notes_row if axis == 0 else notes_col
-        t = lax.rem(own + d, 4)
+    def send_row_note(t, up):
+        return pltpu.make_async_remote_copy(
+            src_ref=notes_row.at[t], dst_ref=notes_row.at[t],
+            send_sem=row_notes_send.at[up, t], recv_sem=row_notes_recv.at[t],
+            device_id={"row": lax.rem(z + (1 if up else 3), 4)}, device_id_type=MESH,
+        )
+
+    def send_note(d):
+        return pltpu.make_async_remote_copy(
+            src_ref=note, dst_ref=notes_col.at[j],
+            send_sem=notes_send.at[d], recv_sem=notes_recv.at[j],
+            device_id={"col": lax.rem(j + d, 4)}, device_id_type=MESH,
+        )
+
+    def got_note(d):
+        t = lax.rem(j + d, 4)
         pltpu.make_async_remote_copy(
-            src_ref=note, dst_ref=held.at[t],
-            send_sem=notes_send.at[axis, d], recv_sem=notes_recv.at[axis, t],
-            device_id={"row" if axis == 0 else "col": t}, device_id_type=MESH,
+            src_ref=note, dst_ref=notes_col.at[t],
+            send_sem=notes_send.at[d], recv_sem=notes_recv.at[t],
+            device_id={"col": t}, device_id_type=MESH,
         ).wait_recv()
 
-    pl.semaphore_wait(barrier, 6)
-    for axis in range(2):
-        for d in range(1, 4):
-            send_note(d, axis).start()
+    pl.semaphore_wait(barrier, 3 + jnp.minimum(z, 1))
+
+    @pl.when(z > 0)
+    def _():
+        pl.semaphore_signal(barrier, inc=1, device_id={"row": z - 1}, device_id_type=MESH)
+        send_row_note(z, 0).start()
+
+    @pl.when(z < 3)
+    def _():
+        pl.semaphore_signal(barrier, inc=1, device_id={"row": z + 1}, device_id_type=MESH)
+
+    for d in range(1, 4):
+        send_note(d).start()
 
     for load in right_loads:
         load.wait()
     for n in range(CAP):
         right_held[z, n] = right_full[right_blocks[0, 0, n]]
-        if n < AHEAD:
-            send_own(n)
+
+        @pl.when(z > 0)
+        def _():
+            send_right(z, n, 0).start()
+
+    @pl.when(z < 3)
+    def _():
+        pl.semaphore_wait(barrier, 1)
+        send_row_note(z, 1).start()
+        for n in range(CAP):
+            send_right(z, n, 1).start()
 
     for load in left_loads:
         load.wait()
@@ -217,12 +227,27 @@
                 def _():
                     send_right(z + d, b, 0).start()
 
+    def take_note(d):
+        for up in (1, 0):
+            t = z - d if up else z + d
+
+            @pl.when((z >= d) if up else (z + d < 4))
+            def _():
+                send_row_note(t, up).wait_recv()
+                if d < 3:
+
+                    @pl.when((z < 3) if up else (z > 0))
+                    def _():
+                        send_row_note(t, up).start()
+
+                read = pltpu.make_async_copy(notes_row.at[t], read_row.at[t], note_sem.at[0])
+                read.start()
+                read.wait()
+
+    take_note(1)
+
     def first(b, carry):
         take_right(1, b)
-
-        @pl.when(b + AHEAD < CAP)
-        def _():
-            send_own(b + AHEAD)
 
         got_left(partner, b)
         pass_left(b).start()
@@ -237,17 +262,12 @@
         return carry
 
     lax.fori_loop(0, CAP, rest_of_left, 0)
-    for axis in range(2):
-        for d in range(1, 4):
-            got_note(d, axis)
-    reads = (
-        pltpu.make_async_copy(notes_row, read_row, note_sem.at[0]),
-        pltpu.make_async_copy(notes_col, read_col, note_sem.at[1]),
-    )
-    for read in reads:
-        read.start()
-    for read in reads:
-        read.wait()
+    for d in range(1, 4):
+        got_note(d)
+    read = pltpu.make_async_copy(notes_col, read_col, note_sem.at[1])
+    read.start()
+    read.wait()
+    take_note(2)
 
     def second(b, carry):
         take_right(2, b)
@@ -274,6 +294,7 @@
 
         return carry
 
+    take_note(3)
     lax.fori_loop(0, CAP, third, 0)
 
     def sent(b, carry):
@@ -293,9 +314,17 @@
         return carry
 
     lax.fori_loop(0, CAP, sent, 0)
-    for axis in range(2):
-        for d in range(1, 4):
-            send_note(d, axis).wait_send()
+    for d in range(1, 4):
+        send_note(d).wait_send()
+    for d in range(3):
+
+        @pl.when((z >= d) & (z < 3))
+        def _():
+            send_row_note(z - d, 1).wait_send()
+
+        @pl.when((z + d < 4) & (z > 0))
+        def _():
+            send_row_note(z + d, 0).wait_send()
 
 
 def packed_lines(left_tiles, right_tiles, left_blocks, left_count, right_blocks, right_count):
@@ -329,7 +358,9 @@
             dma((3, CAP)),
             dma((4, CAP)),
             dma((2, 4)),
-            dma((2, 4)),
+            dma((4,)),
+            dma((4,)),
+            dma((4,)),
         ],
         compiler_params=pltpu.CompilerParams(
             collective_id=0, has_side_effects=True, vmem_limit_bytes=56 * 1024 * 1024

time: 44.8 us -> 44.5 us (level)
  no operation moved by 1% of the time
where the time goes in v3:
time: 44.5 us; the launch traced here: 44.3 us
  Pallas kernels  41.9 us (94%)
  between operations  1.3 us (3%)
  local copies, waits for them, and re-layouts  1.15 us (3%)
    pallas_call x1, Pallas kernels, packed_lines(): pl.pallas_call(kernel, out_shape=pltpu.VMEM((rows, cols), jnp.float32), i...  41.9 us
    unnamed x1, local copies, waits for them, and re-layouts  1.15 us

profile of v3, /device:TPU:0, one launch (start us, length us, event | category | flops | bytes accessed | tf_op | source)
XLA Modules:
  0.0 44.3 jit_solution(140063492420665813)
XLA Ops:
  1.3 41.9 %shard_map.64 = f32[512,768]{1,0:T(8,128)S(1)} custom-call(bf16[512,1280]{1,0:T(8,128)(2,1)} %left_ref.1, bf16[1280,768]{1,0:T(8,128)(2,1)} %right_ref.1, s32[1,1,10]{2,1,0:T(1,128)} %left_blocks.1, s32[1,1]{1,0:T(1,128)S(6)} %copy.9.left_count, s32[1,1,15]{2,1,0:T(1,128)} %right_blocks.1, s32[1,1]{1,0:T(1,128)S(6)} %copy.10.right_count), custom_call_target="tpu_custom_call" | custom-call | flops 1073741824 | bytes 5242880 | tf_op jit(solution)/shard_map/pallas_call | solution.py:336
  43.2 1.1 %copy.8 = f32[512,768]{1,0:T(8,128)} copy(f32[512,768]{1,0:T(8,128)S(1)} %shard_map.64) | data formatting | bytes 3145728

commit v4 on v2

--- a/solution.py
+++ b/solution.py
@@ -232,6 +232,7 @@
     lax.fori_loop(0, CAP, first, 0)
 
     def rest_of_left(b, carry):
+        take_right(2, b)
         got_left(sibling, b)
         got_left(far, b)
         return carry
@@ -250,8 +251,6 @@
         read.wait()
 
     def second(b, carry):
-        take_right(2, b)
-
         @pl.when(z > 0)
         def _():
             add(z - 1, b, False)

time: 44.8 us -> 44.8 us (level)
  no operation moved by 1% of the time
where the time goes in v4:
time: 44.8 us; the launch traced here: 44.6 us
  Pallas kernels  42.2 us (94%)
  between operations  1.3 us (3%)
  local copies, waits for them, and re-layouts  1.15 us (3%)
    pallas_call x1, Pallas kernels, packed_lines(): pl.pallas_call(kernel, out_shape=pltpu.VMEM((rows, cols), jnp.float32), i...  42.2 us
    unnamed x1, local copies, waits for them, and re-layouts  1.15 us

profile of v4, /device:TPU:0, one launch (start us, length us, event | category | flops | bytes accessed | tf_op | source)
XLA Modules:
  0.0 44.6 jit_solution(14662323676201387138)
XLA Ops:
  1.3 42.2 %shard_map.64 = f32[512,768]{1,0:T(8,128)S(1)} custom-call(bf16[512,1280]{1,0:T(8,128)(2,1)} %left_ref.1, bf16[1280,768]{1,0:T(8,128)(2,1)} %right_ref.1, s32[1,1,10]{2,1,0:T(1,128)} %left_blocks.1, s32[1,1]{1,0:T(1,128)S(6)} %copy.9.left_count, s32[1,1,15]{2,1,0:T(1,128)} %right_blocks.1, s32[1,1]{1,0:T(1,128)S(6)} %copy.10.right_count), custom_call_target="tpu_custom_call" | custom-call | flops 1073741824 | bytes 5242880 | tf_op jit(solution)/shard_map/pallas_call | solution.py:306
  43.5 1.1 %copy.8 = f32[512,768]{1,0:T(8,128)} copy(f32[512,768]{1,0:T(8,128)S(1)} %shard_map.64) | data formatting | bytes 3145728
